TPU v7x, 512 devices: a whole 4x8x8 slice. The times are simulated.
512 devices in a mesh: span: 32 (over z, x), sub: 16 (over y, core).
Axes of the slice: x: 4, y: 8, z: 8, core: 2. Of those that a mesh axis runs over, the one named last changes fastest.
Arguments:
- stress: bfloat16 [512, 768, 128], P(('span', 'sub')), may hold values from -6 to 6
- history: float32 [8, 512, 768], P(None, ('span', 'sub')), may hold values from -6 to 6
- retard: float32 [8], replicated, may hold values from 0.3 to 30
- compliance: float32 [8], replicated, may hold values from 0.2 to 2
- micro: float32 [512, 768], P(('span', 'sub')), may hold values from 0.5 to 5
- lengths: int32 [512], P(('span', 'sub')), may hold values from 1 to 768, 131072 in all
- multiplier_index: int32 [512, 768], P(('span', 'sub')), may hold values from 0 to 131071, as said below
- dual_block: bfloat16 [512, 768, 768], P(('span', 'sub')), may hold values from -1 to 4, as said below
- corner_map: bfloat16 [512, 768, 128], P(('span', 'sub')), may hold values from -0.21875 to 0.21875
- coarse_stiffness_inverse: float32 [32, 128, 128], P('span'), may hold values from -1 to 4, as said below
Outputs:
- solution: float32 [131072, 128], P(('span', 'sub'))
- residual: float32 [131072, 128], P(('span', 'sub'))
Inputs may be any that keep to these rules, and one draw needn't show every extreme that they name: `multiplier_index`: each slot of a subdomain names a multiplier held by its own device or by the device of the same sub index in one of the two neighbouring spans; multipliers 0 and 131071 are named in every draw. `dual_block`: each block is symmetric with a diagonal between 1 and 4. `coarse_stiffness_inverse`: each span's matrix is symmetric with a diagonal between 1 and 4.
All inputs are finite; a program needn't handle non-finite values. No bound on the sum of `lengths` on one device may be relied on, other than what follows from the above.
Results may differ from a plain program's by a relative error of at most 0.024.
Values may be sent and summed in bfloat16 or wider, within the bound.
A program may use at most 64 MiB of HBM per device.

v0:
```python
import jax
import jax.numpy as jnp
from jax import lax
from jax.sharding import PartitionSpec as P

ITERS = 2


def from_behind(shard, axis, by):
    size = lax.axis_size(axis)
    pairs = [(i, i + by) for i in range(size) if 0 <= i + by < size]
    return lax.ppermute(shard, axis, pairs)


def padded(shard, sides, width):
    for axis, dim in sides:
        size, length = (lax.axis_size(axis), shard.shape[dim])
        up = [(i, (i + 1) % size) for i in range(size - 1)]
        down = [(j, i) for i, j in up]
        last = lax.slice_in_dim(shard, length - width, length, axis=dim)
        leading = lax.slice_in_dim(shard, 0, width, axis=dim)
        before = lax.ppermute(last, axis, up)
        after = lax.ppermute(leading, axis, down)
        shard = jnp.concatenate([before, shard, after], axis=dim)
    return shard


def column_sums(left, right):
    return jnp.sum(left * right, axis=0)


def on_device(
    stress,
    history,
    retard,
    compliance,
    micro,
    lengths,
    multiplier_index,
    dual_block,
    corner_map,
    coarse_stiffness_inverse,
):
    sub_count = dual_block.shape[0]
    width = dual_block.shape[1]
    loads = stress.shape[2]
    owned = sub_count * width // 3
    groups = lax.axis_size("sub")
    here = lax.axis_index("span")
    live = (jnp.arange(width)[None, :] < lengths[:, None]).astype(jnp.float32)
    owner_dev = multiplier_index // owned
    window_pos = ((owner_dev // groups - here + 1) * owned + multiplier_index % owned).reshape(-1)
    weight_k = 1.0 - jnp.exp(-1.0 / retard)
    creep = jnp.sum(weight_k * compliance)
    past = jnp.sum(weight_k[:, None, None] * history, axis=0)
    relaxed = micro / (1.0 + micro)
    load = (
        (creep + 0.5 * relaxed[:, :, None]) * stress.astype(jnp.float32) - past[:, :, None]
    ) * live[:, :, None]

    def assemble(local):
        window = (
            jnp.zeros((3 * owned, loads), jnp.float32).at[window_pos].add(local.reshape(-1, loads))
        )
        from_next = from_behind(window[:owned], "span", -1)
        from_prev = from_behind(window[2 * owned :], "span", 1)
        return window[owned : 2 * owned] + from_next + from_prev

    kernel = coarse_stiffness_inverse[0]
    rhs = assemble(load)
    solution = jnp.zeros_like(rhs)
    residual = rhs
    direction = rhs
    norm_now = lax.psum(column_sums(residual, residual), ("span", "sub"))
    for step in range(ITERS):
        narrow = direction.astype(jnp.bfloat16)
        apply_window = padded(narrow, (("span", 0),), owned)
        gathered = (
            apply_window[window_pos].reshape(sub_count, width, loads).astype(jnp.float32)
            * live[:, :, None]
        ).astype(jnp.bfloat16)
        apply_local = jnp.einsum(
            "smn,snr->smr", dual_block, gathered, preferred_element_type=jnp.float32
        )
        corner_part = jnp.einsum(
            "smc,smr->cr", corner_map, gathered, preferred_element_type=jnp.float32
        )
        corner_residual = lax.psum(corner_part.astype(jnp.bfloat16), "sub").astype(jnp.float32)
        corner_update = jnp.dot(kernel, corner_residual, precision=lax.Precision.HIGHEST)
        spread_corners = jnp.einsum(
            "smc,cr->smr",
            corner_map,
            corner_update.astype(jnp.bfloat16),
            preferred_element_type=jnp.float32,
        )
        image = assemble((apply_local + spread_corners) * live[:, :, None])
        curve = lax.psum(column_sums(direction, image), ("span", "sub"))
        alpha = norm_now / curve
        solution = solution + alpha * direction
        residual = residual - alpha * image
        norm_next = lax.psum(column_sums(residual, residual), ("span", "sub"))
        direction = residual + norm_next / norm_now * direction
        norm_now = norm_next
    return (solution, residual)


def solution(mesh):
    placed = (
        P(("span", "sub"), None, None),
        P(None, ("span", "sub"), None),
        P(),
        P(),
        P(("span", "sub"), None),
        P(("span", "sub")),
        P(("span", "sub"), None),
        P(("span", "sub"), None, None),
        P(("span", "sub"), None, None),
        P("span", None, None),
    )
    return jax.shard_map(
        on_device,
        mesh=mesh,
        in_specs=placed,
        out_specs=(P(("span", "sub"), None), P(("span", "sub"), None)),
        check_vma=False,
    )
```

profile of v0, /device:TPU:10, one launch (start us, length us, event | category | flops | bytes accessed | tf_op | source)
XLA Modules:
  0.0 476.3 jit_solution(13964561409451314039)
XLA Ops:
  1.4 1.3 multiply_reduce_fusion.5
  3.4 0.8 multiply_reduce_fusion.4
  4.3 1.4 fusion.46
  5.6 6.9 %scatter_custom_fusion = f32[768,128]{1,0:T(8,128)S(1)} fusion(s32[768]{0:T(1024)S(1)} %fusion.43, bf16[1,768,128]{2,1,0:T(8,128)(2,1)} %param.10, f32[768]{0:T(1024)S(1)} %fusion.41, f32[768]{0:T(1024)S(1)} %multiply_reduce_fusion.4, f32[768]{0:T(1024)S(1)} %fusion.46, f32[]{:T(128)} %constant.45.clone.1), kind=kCustom, calls=%fused_computation.25 | custom fusion | flops 491520 | bytes 602116 | tf_op jit(solution)/shard_map/scatter-add | solution.py:63
  12.5 2.4 collective-permute-start
  15.0 3.4 collective-permute-start.1
  18.4 1.3 collective-permute-done
  19.6 2.2 collective-permute-done.1
  21.9 2.1 collective-permute-start.3
  23.9 3.9 collective-permute-start.2
  28.2 1.9 collective-permute-done.2
  30.1 1.9 gather_fusion
  32.4 48.7 %psum.43 = bf16[128,128]{0,1:T(8,128)(2,1)S(1)} all-reduce(bf16[128,128]{0,1:T(8,128)(2,1)S(1)} %fusion.8), channel_id=1, replica_groups=mesh['span'=32,'sub'=16] {'sub'}, use_global_device_ids=true, to_apply=%region_5.6 | all-reduce | flops 16384 | bytes 65536 | tf_op jit(solution)/shard_map/psum | solution.py:88
  82.4 6.1 %scatter_custom_fusion.1 = f32[768,128]{1,0:T(8,128)S(1)} fusion(s32[768]{0:T(1024)S(1)} %fusion.43, f32[768,128]{1,0:T(8,128)S(1)} %copy.14, f32[]{:T(128)} %constant.45.clone.1), kind=kCustom, calls=%fused_computation.44 | custom fusion | flops 98304 | bytes 393220 | tf_op jit(solution)/shard_map/scatter-add | solution.py:63
  88.6 1.9 collective-permute-start.4
  90.5 3.9 collective-permute-start.5
  94.4 1.0 collective-permute-done.4
  95.4 1.9 collective-permute-done.5
  97.4 108.1 %all-reduce = (f32[128]{0:T(128)S(1)}, f32[128]{0:T(128)S(1)}) all-reduce(f32[128]{0:T(128)S(1)} %get-tuple-element.3, f32[128]{0:T(128)S(1)} %get-tuple-element.2), channel_id=1, replica_groups=mesh['span'=32,'sub'=16] {'span','sub'}, use_global_device_ids=true, to_apply=%region_4.5 | all-reduce | flops 256 | bytes 2048 | tf_op jit(solution)/shard_map/psum | solution.py:74
  205.6 94.5 %psum.45 = f32[128]{0:T(128)S(1)} all-reduce(f32[128]{0:T(128)S(1)} %multiply_reduce_fusion.1), channel_id=1, replica_groups=mesh['span'=32,'sub'=16] {'span','sub'}, use_global_device_ids=true, to_apply=%region_10.11 | all-reduce | flops 128 | bytes 1024 | tf_op jit(solution)/shard_map/psum | solution.py:101
  300.2 2.8 collective-permute-start.7
  302.9 3.1 collective-permute-start.6
  306.3 2.8 collective-permute-done.6
  309.1 1.9 gather_fusion.1
  312.0 42.7 %psum.46 = bf16[128,128]{0,1:T(8,128)(2,1)S(1)} all-reduce(bf16[128,128]{0,1:T(8,128)(2,1)S(1)} %fusion.9), channel_id=1, replica_groups=mesh['span'=32,'sub'=16] {'sub'}, use_global_device_ids=true, to_apply=%region_11.12 | all-reduce | flops 16384 | bytes 65536 | tf_op jit(solution)/shard_map/psum | solution.py:88
  355.3 6.1 %scatter_custom_fusion.2 = f32[768,128]{1,0:T(8,128)S(1)} fusion(s32[768]{0:T(1024)S(1)} %fusion.43, f32[768,128]{1,0:T(8,128)S(1)} %copy.15, f32[]{:T(128)} %constant.45.clone.1), kind=kCustom, calls=%fused_computation.42 | custom fusion | flops 98304 | bytes 393220 | tf_op jit(solution)/shard_map/scatter-add | solution.py:63
  361.5 1.9 collective-permute-start.8
  363.4 3.9 collective-permute-start.9
  367.3 1.0 collective-permute-done.8
  368.4 1.9 collective-permute-done.9
  370.3 105.2 %psum.47 = f32[128]{0:T(128)S(1)} all-reduce(f32[128]{0:T(128)S(1)} %multiply_reduce_fusion), channel_id=1, replica_groups=mesh['span'=32,'sub'=16] {'span','sub'}, use_global_device_ids=true, to_apply=%region_14.15 | all-reduce | flops 128 | bytes 1024 | tf_op jit(solution)/shard_map/psum | solution.py:97
  475.6 0.8 multiply_subtract_fusion
  (34 shorter events, 4.8 us)
Async XLA Ops:
  0.6 80.5 %copy-start = (bf16[1,768,768]{2,1,0:T(8,128)(2,1)S(1)}, bf16[1,768,768]{2,1,0:T(8,128)(2,1)}, u32[]{:S(2)}) copy-start(bf16[1,768,768]{2,1,0:T(8,128)(2,1)} %param.17) | copy-start | bytes 3538948
  12.5 7.1 %collective-permute-start = (f32[256,128]{1,0:T(8,128)S(1)}, f32[256,128]{1,0:T(8,128)S(1)}, u32[]{:S(2)}, u32[]{:S(2)}) collective-permute-start(f32[256,128]{1,0:T(8,128)S(1)} %get-tuple-element.15), channel_id=1, source_target_pairs={{16,0},{32,16},{48,32},{64,48},{80,64},{96,80},{112,96},{128,112},... | collective-permute-start | bytes 393224 | tf_op jit(solution)/shard_map/ppermute | solution.py:12
  15.0 6.9 %collective-permute-start.1 = (f32[256,128]{1,0:T(8,128)S(1)}, f32[256,128]{1,0:T(8,128)S(1)}, u32[]{:S(2)}, u32[]{:S(2)}) collective-permute-start(f32[256,128]{1,0:T(8,128)S(1)} %get-tuple-element.16), channel_id=1, source_target_pairs={{0,16},{16,32},{32,48},{48,64},{64,80},{80,96},{96,112},{112,128},... | collective-permute-start | bytes 393224 | tf_op jit(solution)/shard_map/ppermute | solution.py:12
  21.9 10.1 %copy-start.1 = (bf16[1,768,128]{2,1,0:T(8,128)(2,1)S(1)}, bf16[1,768,128]{2,1,0:T(8,128)(2,1)}, u32[]{:S(2)}) copy-start(bf16[1,768,128]{2,1,0:T(8,128)(2,1)} %param.18) | copy-start | bytes 589828
  21.9 6.3 %collective-permute-start.3 = (bf16[256,128]{1,0:T(8,128)(2,1)S(1)}, bf16[256,128]{1,0:T(8,128)(2,1)S(1)}, u32[]{:S(2)}, u32[]{:S(2)}) collective-permute-start(bf16[256,128]{1,0:T(8,128)(2,1)S(1)} %get-tuple-element.7), channel_id=1, source_target_pairs={{16,0},{32,16},{48,32},{64,48},{80,64},{96,80},{112,96},{128,112},... | collective-permute-start | bytes 196616 | tf_op jit(solution)/shard_map/ppermute | solution.py:23
  23.9 6.2 %collective-permute-start.2 = (bf16[256,128]{1,0:T(8,128)(2,1)S(1)}, bf16[256,128]{1,0:T(8,128)(2,1)S(1)}, u32[]{:S(2)}, u32[]{:S(2)}) collective-permute-start(bf16[256,128]{1,0:T(8,128)(2,1)S(1)} %get-tuple-element.7), channel_id=1, source_target_pairs={{0,16},{16,32},{32,48},{48,64},{64,80},{80,96},{96,112},{112,128},... | collective-permute-start | bytes 196616 | tf_op jit(solution)/shard_map/ppermute | solution.py:22
  32.0 49.8 %copy-start.2 = (f32[1,128,128]{2,1,0:T(8,128)S(1)}, f32[1,128,128]{2,1,0:T(8,128)}, u32[]{:S(2)}) copy-start(f32[1,128,128]{2,1,0:T(8,128)} %param.19) | copy-start | bytes 196612
  88.6 6.9 %collective-permute-start.4 = (f32[256,128]{1,0:T(8,128)S(1)}, f32[256,128]{1,0:T(8,128)S(1)}, u32[]{:S(2)}, u32[]{:S(2)}) collective-permute-start(f32[256,128]{1,0:T(8,128)S(1)} %get-tuple-element.13), channel_id=1, source_target_pairs={{16,0},{32,16},{48,32},{64,48},{80,64},{96,80},{112,96},{128,112},... | collective-permute-start | bytes 393224 | tf_op jit(solution)/shard_map/ppermute | solution.py:12
  90.5 6.9 %collective-permute-start.5 = (f32[256,128]{1,0:T(8,128)S(1)}, f32[256,128]{1,0:T(8,128)S(1)}, u32[]{:S(2)}, u32[]{:S(2)}) collective-permute-start(f32[256,128]{1,0:T(8,128)S(1)} %get-tuple-element.14), channel_id=1, source_target_pairs={{0,16},{16,32},{32,48},{48,64},{64,80},{80,96},{96,112},{112,128},... | collective-permute-start | bytes 393224 | tf_op jit(solution)/shard_map/ppermute | solution.py:12
  300.2 6.2 %collective-permute-start.7 = (bf16[256,128]{1,0:T(8,128)(2,1)S(1)}, bf16[256,128]{1,0:T(8,128)(2,1)S(1)}, u32[]{:S(2)}, u32[]{:S(2)}) collective-permute-start(bf16[256,128]{1,0:T(8,128)(2,1)S(1)} %fusion.47), channel_id=1, source_target_pairs={{16,0},{32,16},{48,32},{64,48},{80,64},{96,80},{112,96},{128,112},... | collective-permute-start | bytes 196616 | tf_op jit(solution)/shard_map/ppermute | solution.py:23
  302.9 6.2 %collective-permute-start.6 = (bf16[256,128]{1,0:T(8,128)(2,1)S(1)}, bf16[256,128]{1,0:T(8,128)(2,1)S(1)}, u32[]{:S(2)}, u32[]{:S(2)}) collective-permute-start(bf16[256,128]{1,0:T(8,128)(2,1)S(1)} %fusion.47), channel_id=1, source_target_pairs={{0,16},{16,32},{32,48},{48,64},{64,80},{80,96},{96,112},{112,128},... | collective-permute-start | bytes 196616 | tf_op jit(solution)/shard_map/ppermute | solution.py:22
  361.5 6.9 %collective-permute-start.8 = (f32[256,128]{1,0:T(8,128)S(1)}, f32[256,128]{1,0:T(8,128)S(1)}, u32[]{:S(2)}, u32[]{:S(2)}) collective-permute-start(f32[256,128]{1,0:T(8,128)S(1)} %get-tuple-element.11), channel_id=1, source_target_pairs={{16,0},{32,16},{48,32},{64,48},{80,64},{96,80},{112,96},{128,112},... | collective-permute-start | bytes 393224 | tf_op jit(solution)/shard_map/ppermute | solution.py:12
  363.4 6.9 %collective-permute-start.9 = (f32[256,128]{1,0:T(8,128)S(1)}, f32[256,128]{1,0:T(8,128)S(1)}, u32[]{:S(2)}, u32[]{:S(2)}) collective-permute-start(f32[256,128]{1,0:T(8,128)S(1)} %get-tuple-element.12), channel_id=1, source_target_pairs={{0,16},{16,32},{32,48},{48,64},{64,80},{80,96},{96,112},{112,128},... | collective-permute-start | bytes 393224 | tf_op jit(solution)/shard_map/ppermute | solution.py:12
where the time goes:
time: 477 us; the launch traced here: 476 us
  blocking collectives  399 us (84%)
  starting transfers between devices  29.4 us (6%)
  other arithmetic  24.3 us (5%)
  waiting for transfers between devices  14.6 us (3%)
    psum x1, blocking collectives, on_device(): norm_now = lax.psum(column_sums(residual, residual), ('span', 'sub'))  108 us
    psum x1, blocking collectives, on_device(): curve = lax.psum(column_sums(direction, image), ('span', 'sub'))  105 us
    psum x1, blocking collectives, on_device(): norm_next = lax.psum(column_sums(residual, residual), ('span', 'sub'))  94.5 us
    psum x2, blocking collectives, on_device(): lax.psum(corner_part.astype(jnp.bfloat16), 'sub').astype(jnp.float32)  91.4 us
    scatter-add x3, other arithmetic, assemble(): jnp.zeros((3 * owned, loads), jnp.float32).at[window_pos]  19.1 us
    ppermute x6, starting transfers between devices, from_behind(): return lax.ppermute(shard, axis, pairs)  17.5 us
  transfers between devices with their start and end apart: 10, of which 10 were waited for; matrix products, arithmetic and copies ran while one was open for 0% of the time, Pallas kernels for 0%

commit v1 on v0

--- a/solution.py
+++ b/solution.py
@@ -85,7 +85,9 @@
         corner_part = jnp.einsum(
             "smc,smr->cr", corner_map, gathered, preferred_element_type=jnp.float32
         )
-        corner_residual = lax.psum(corner_part.astype(jnp.bfloat16), "sub").astype(jnp.float32)
+        corner_residual = jnp.sum(
+            lax.all_gather(corner_part.astype(jnp.bfloat16), "sub"), axis=0
+        ).astype(jnp.float32)
         corner_update = jnp.dot(kernel, corner_residual, precision=lax.Precision.HIGHEST)
         spread_corners = jnp.einsum(
             "smc,cr->smr",

time: 477 us -> 431 us (0.904)
  the two profiles are of different devices: /device:TPU:10 before, /device:TPU:1 now
where the time goes in v1:
time: 431 us
  blocking collectives  357 us (83%)
  starting transfers between devices  25.8 us (6%)
  other arithmetic  24.9 us (6%)
  waiting for transfers between devices  14.1 us (3%)
  local copies, waits for them, and re-layouts  4.37 us (1%)
    psum x1, blocking collectives, on_device(): norm_now = lax.psum(column_sums(residual, residual), ('span', 'sub'))  112 us
    psum x1, blocking collectives, on_device(): curve = lax.psum(column_sums(direction, image), ('span', 'sub'))  106 us
    psum x1, blocking collectives, on_device(): norm_next = lax.psum(column_sums(residual, residual), ('span', 'sub'))  94.4 us
    all_gather x2, blocking collectives, on_device(): lax.all_gather(corner_part.astype(jnp.bfloat16), 'sub')  44.6 us
    scatter-add x3, other arithmetic, assemble(): jnp.zeros((3 * owned, loads), jnp.float32).at[window_pos]  19.1 us
    ppermute x6, starting transfers between devices, from_behind(): return lax.ppermute(shard, axis, pairs)  16.4 us
  transfers between devices with their start and end apart: 10, of which 8 were waited for; matrix products, arithmetic and copies ran while one was open for 0% of the time, Pallas kernels for 0%

profile of v1, /device:TPU:1, one launch (start us, length us, event | category | flops | bytes accessed | tf_op | source)
XLA Modules:
  0.0 430.6 jit_solution(13277407826748545491)
XLA Ops:
  1.4 0.7 fusion.43
  2.1 1.3 multiply_reduce_fusion.5
  3.4 1.3 fusion.46
  4.8 0.8 multiply_reduce_fusion.4
  5.6 6.9 %scatter_custom_fusion = f32[768,128]{1,0:T(8,128)S(1)} fusion(s32[768]{0:T(1024)S(1)} %fusion.43, bf16[1,768,128]{2,1,0:T(8,128)(2,1)} %param.10, f32[768]{0:T(1024)S(1)} %fusion.41, f32[768]{0:T(1024)S(1)} %multiply_reduce_fusion.4, f32[768]{0:T(1024)S(1)} %fusion.46, f32[]{:T(128)} %constant.47.clone.1), kind=kCustom, calls=%fused_computation.27 | custom fusion | flops 491520 | bytes 602116 | tf_op jit(solution)/shard_map/scatter-add | solution.py:63
  12.5 1.3 collective-permute-start
  13.8 4.6 %collective-permute-start.1 = (f32[256,128]{1,0:T(8,128)S(1)}, f32[256,128]{1,0:T(8,128)S(1)}, u32[]{:S(2)}, u32[]{:S(2)}) collective-permute-start(f32[256,128]{1,0:T(8,128)S(1)} %get-tuple-element.16), channel_id=1, source_target_pairs={{0,16},{16,32},{32,48},{48,64},{64,80},{80,96},{96,112},{112,128},... | collective-permute-start | bytes 393224 | tf_op jit(solution)/shard_map/ppermute | solution.py:12
  18.8 1.5 collective-permute-done.1
  20.4 3.9 collective-permute-start.2
  24.3 1.3 collective-permute-start.3
  25.6 3.7 collective-permute-done.3
  29.3 1.9 gather_fusion
  31.6 24.7 %all-gather = bf16[2048,128]{0,1:T(8,128)(2,1)S(1)} all-gather(bf16[128,128]{0,1:T(8,128)(2,1)S(1)} %fusion.8), channel_id=2, replica_groups=mesh['span'=32,'sub'=16] {'sub'}, dimensions={0}, use_global_device_ids=true | all-gather | bytes 557056 | tf_op jit(solution)/shard_map/all_gather | solution.py:89
  58.0 6.1 %scatter_custom_fusion.1 = f32[768,128]{1,0:T(8,128)S(1)} fusion(s32[768]{0:T(1024)S(1)} %fusion.43, f32[768,128]{1,0:T(8,128)S(1)} %copy.16, f32[]{:T(128)} %constant.47.clone.1), kind=kCustom, calls=%fused_computation.46 | custom fusion | flops 98304 | bytes 393220 | tf_op jit(solution)/shard_map/scatter-add | solution.py:63
  64.1 1.3 collective-permute-start.4
  65.4 4.0 collective-permute-start.5
  69.4 1.5 collective-permute-done.4
  71.0 0.9 collective-permute-done.5
  71.9 112.2 %all-reduce = (f32[128]{0:T(128)S(1)}, f32[128]{0:T(128)S(1)}) all-reduce(f32[128]{0:T(128)S(1)} %get-tuple-element.3, f32[128]{0:T(128)S(1)} %get-tuple-element.2), channel_id=1, replica_groups=mesh['span'=32,'sub'=16] {'span','sub'}, use_global_device_ids=true, to_apply=%region_4.5 | all-reduce | flops 256 | bytes 2048 | tf_op jit(solution)/shard_map/psum | solution.py:74
  184.1 94.4 %psum.30 = f32[128]{0:T(128)S(1)} all-reduce(f32[128]{0:T(128)S(1)} %multiply_reduce_fusion.1), channel_id=1, replica_groups=mesh['span'=32,'sub'=16] {'span','sub'}, use_global_device_ids=true, to_apply=%region_10.11 | all-reduce | flops 128 | bytes 1024 | tf_op jit(solution)/shard_map/psum | solution.py:103
  278.6 2.8 collective-permute-start.6
  281.4 1.3 collective-permute-start.7
  282.7 3.7 collective-permute-done.7
  286.5 1.9 gather_fusion.1
  289.4 19.9 %all-gather.1 = bf16[2048,128]{0,1:T(8,128)(2,1)S(1)} all-gather(bf16[128,128]{0,1:T(8,128)(2,1)S(1)} %fusion.9), channel_id=3, replica_groups=mesh['span'=32,'sub'=16] {'sub'}, dimensions={0}, use_global_device_ids=true | all-gather | bytes 557056 | tf_op jit(solution)/shard_map/all_gather | solution.py:89
  310.3 6.1 %scatter_custom_fusion.2 = f32[768,128]{1,0:T(8,128)S(1)} fusion(s32[768]{0:T(1024)S(1)} %fusion.43, f32[768,128]{1,0:T(8,128)S(1)} %copy.17, f32[]{:T(128)} %constant.47.clone.1), kind=kCustom, calls=%fused_computation.44 | custom fusion | flops 98304 | bytes 393220 | tf_op jit(solution)/shard_map/scatter-add | solution.py:63
  316.4 1.3 collective-permute-start.8
  317.8 4.0 collective-permute-start.9
  321.8 1.5 collective-permute-done.8
  323.3 0.9 collective-permute-done.9
  324.2 105.6 %psum.31 = f32[128]{0:T(128)S(1)} all-reduce(f32[128]{0:T(128)S(1)} %multiply_reduce_fusion), channel_id=1, replica_groups=mesh['span'=32,'sub'=16] {'span','sub'}, use_global_device_ids=true, to_apply=%region_14.15 | all-reduce | flops 128 | bytes 1024 | tf_op jit(solution)/shard_map/psum | solution.py:99
  429.8 0.8 multiply_subtract_fusion
  (38 shorter events, 4.7 us)
Async XLA Ops:
  0.6 56.1 %copy-start = (bf16[1,768,768]{2,1,0:T(8,128)(2,1)S(1)}, bf16[1,768,768]{2,1,0:T(8,128)(2,1)}, u32[]{:S(2)}) copy-start(bf16[1,768,768]{2,1,0:T(8,128)(2,1)} %param.17) | copy-start | bytes 3538948
  12.5 6.3 %collective-permute-start = (f32[256,128]{1,0:T(8,128)S(1)}, f32[256,128]{1,0:T(8,128)S(1)}, u32[]{:S(2)}, u32[]{:S(2)}) collective-permute-start(f32[256,128]{1,0:T(8,128)S(1)} %get-tuple-element.15), channel_id=1, source_target_pairs={{16,0},{32,16},{48,32},{64,48},{80,64},{96,80},{112,96},{128,112},... | collective-permute-start | bytes 393224 | tf_op jit(solution)/shard_map/ppermute | solution.py:12
  13.8 6.5 %collective-permute-start.1 = (f32[256,128]{1,0:T(8,128)S(1)}, f32[256,128]{1,0:T(8,128)S(1)}, u32[]{:S(2)}, u32[]{:S(2)}) collective-permute-start(f32[256,128]{1,0:T(8,128)S(1)} %get-tuple-element.16), channel_id=1, source_target_pairs={{0,16},{16,32},{32,48},{48,64},{64,80},{80,96},{96,112},{112,128},... | collective-permute-start | bytes 393224 | tf_op jit(solution)/shard_map/ppermute | solution.py:12
  20.4 10.8 %copy-start.1 = (bf16[1,768,128]{2,1,0:T(8,128)(2,1)S(1)}, bf16[1,768,128]{2,1,0:T(8,128)(2,1)}, u32[]{:S(2)}) copy-start(bf16[1,768,128]{2,1,0:T(8,128)(2,1)} %param.18) | copy-start | bytes 589828
  20.4 5.2 %collective-permute-start.2 = (bf16[256,128]{1,0:T(8,128)(2,1)S(1)}, bf16[256,128]{1,0:T(8,128)(2,1)S(1)}, u32[]{:S(2)}, u32[]{:S(2)}) collective-permute-start(bf16[256,128]{1,0:T(8,128)(2,1)S(1)} %get-tuple-element.7), channel_id=1, source_target_pairs={{0,16},{16,32},{32,48},{48,64},{64,80},{80,96},{96,112},{112,128},... | collective-permute-start | bytes 196616 | tf_op jit(solution)/shard_map/ppermute | solution.py:22
  24.3 5.0 %collective-permute-start.3 = (bf16[256,128]{1,0:T(8,128)(2,1)S(1)}, bf16[256,128]{1,0:T(8,128)(2,1)S(1)}, u32[]{:S(2)}, u32[]{:S(2)}) collective-permute-start(bf16[256,128]{1,0:T(8,128)(2,1)S(1)} %get-tuple-element.7), channel_id=1, source_target_pairs={{16,0},{32,16},{48,32},{64,48},{80,64},{96,80},{112,96},{128,112},... | collective-permute-start | bytes 196616 | tf_op jit(solution)/shard_map/ppermute | solution.py:23
  56.4 0.9 copy-start.2
  64.1 6.8 %collective-permute-start.4 = (f32[256,128]{1,0:T(8,128)S(1)}, f32[256,128]{1,0:T(8,128)S(1)}, u32[]{:S(2)}, u32[]{:S(2)}) collective-permute-start(f32[256,128]{1,0:T(8,128)S(1)} %get-tuple-element.13), channel_id=1, source_target_pairs={{16,0},{32,16},{48,32},{64,48},{80,64},{96,80},{112,96},{128,112},... | collective-permute-start | bytes 393224 | tf_op jit(solution)/shard_map/ppermute | solution.py:12
  65.4 6.4 %collective-permute-start.5 = (f32[256,128]{1,0:T(8,128)S(1)}, f32[256,128]{1,0:T(8,128)S(1)}, u32[]{:S(2)}, u32[]{:S(2)}) collective-permute-start(f32[256,128]{1,0:T(8,128)S(1)} %get-tuple-element.14), channel_id=1, source_target_pairs={{0,16},{16,32},{32,48},{48,64},{64,80},{80,96},{96,112},{112,128},... | collective-permute-start | bytes 393224 | tf_op jit(solution)/shard_map/ppermute | solution.py:12
  278.6 4.2 collective-permute-start.6
  281.4 5.0 %collective-permute-start.7 = (bf16[256,128]{1,0:T(8,128)(2,1)S(1)}, bf16[256,128]{1,0:T(8,128)(2,1)S(1)}, u32[]{:S(2)}, u32[]{:S(2)}) collective-permute-start(bf16[256,128]{1,0:T(8,128)(2,1)S(1)} %fusion.47), channel_id=1, source_target_pairs={{16,0},{32,16},{48,32},{64,48},{80,64},{96,80},{112,96},{128,112},... | collective-permute-start | bytes 196616 | tf_op jit(solution)/shard_map/ppermute | solution.py:23
  316.4 6.8 %collective-permute-start.8 = (f32[256,128]{1,0:T(8,128)S(1)}, f32[256,128]{1,0:T(8,128)S(1)}, u32[]{:S(2)}, u32[]{:S(2)}) collective-permute-start(f32[256,128]{1,0:T(8,128)S(1)} %get-tuple-element.11), channel_id=1, source_target_pairs={{16,0},{32,16},{48,32},{64,48},{80,64},{96,80},{112,96},{128,112},... | collective-permute-start | bytes 393224 | tf_op jit(solution)/shard_map/ppermute | solution.py:12
  317.8 6.4 %collective-permute-start.9 = (f32[256,128]{1,0:T(8,128)S(1)}, f32[256,128]{1,0:T(8,128)S(1)}, u32[]{:S(2)}, u32[]{:S(2)}) collective-permute-start(f32[256,128]{1,0:T(8,128)S(1)} %get-tuple-element.12), channel_id=1, source_target_pairs={{0,16},{16,32},{32,48},{48,64},{64,80},{80,96},{96,112},{112,128},... | collective-permute-start | bytes 393224 | tf_op jit(solution)/shard_map/ppermute | solution.py:12
